TPU v7x, 256 devices: a whole 4x4x8 slice. The times are simulated.
256 devices in a mesh: az: 32 (over z_hi, y, x), rad: 8 (over z_lo, core).
Axes of the slice: x: 4, y: 4, z: 8 (z_hi: 2, z_lo: 4; z = z_hi * 4 + z_lo), core: 2. Of those that a mesh axis runs over, the one named last changes fastest.
Arguments:
- density: float32 [2, 2048, 16384], P(None, 'rad', 'az'), may hold values from 0.5 to 2
- mom_r: float32 [2, 2048, 16384], P(None, 'rad', 'az'), may hold values from -1 to 1
- mom_phi: float32 [2, 2048, 16384], P(None, 'rad', 'az'), may hold values from 0.5 to 1.5
- potential_kernel: bfloat16 [64, 2048, 2048], P('az', 'rad'), may hold values from -2 to 2
- force_kernel: bfloat16 [64, 2048, 2048], P('az', 'rad'), may hold values from -2 to 2
Outputs:
- new_density: float32 [2, 2048, 16384], P(None, 'rad', 'az')
- new_mom_r: float32 [2, 2048, 16384], P(None, 'rad', 'az')
- new_mom_phi: float32 [2, 2048, 16384], P(None, 'rad', 'az')
- potential: float32 [2048, 16384], P('rad', 'az')
All inputs are finite; a program needn't handle non-finite values.
Results may differ from a plain program's by a relative error of at most 0.0015.
The roundings to bfloat16 on the way count: a program that leaves them out, or rounds other values in their place, can miss the bound.
Values may be sent and summed in bfloat16 or wider, within the bound.
A program may use at most 128 MiB of HBM per device.

v0:
```python
import math
import jax
import jax.numpy as jnp
from jax import lax
from jax.sharding import PartitionSpec as P

NAZ = 16384
MODES = 64
aspect_sq = 0.0025


def in_blocks(shard, dim, size):
    before, after = (shard.shape[:dim], shard.shape[dim + 1 :])
    return jnp.moveaxis(shard.reshape(*before, size, -1, *after), dim, 0)


def sum_at_owner(shard, axis, dim):
    blocks = in_blocks(shard, dim, lax.axis_size(axis))
    arrived = lax.all_to_all(blocks, axis, split_axis=0, concat_axis=0, tiled=True)
    return arrived.sum(axis=0)


def laid_out(blocks, dim):
    lengths = list(blocks.shape[1:])
    lengths[dim] *= blocks.shape[0]
    return jnp.moveaxis(blocks, 0, dim).reshape(lengths)


def copy_for_each(shard, axis):
    size = lax.axis_size(axis)
    return lax.all_to_all(
        jnp.broadcast_to(shard[None], (size, *shard.shape)), axis, 0, 0, tiled=True
    )


def gathered_copies(shard, axis, dim):
    return laid_out(copy_for_each(shard, axis), dim)


def rows_first(arrays, axis, dims):
    turned = [jnp.moveaxis(a, dim, 0) for a, dim in zip(arrays, dims)]
    both = jnp.concatenate([t.reshape(len(t), -1) for t in turned], axis=1)
    result, at, gathered = (lax.all_gather(both, axis, axis=0, tiled=True), 0, [])
    for t, dim in zip(turned, dims):
        slab = result[:, at : at + t[0].size].reshape(-1, *t.shape[1:])
        gathered.append(jnp.moveaxis(slab, 0, dim))
        at += t[0].size
    return tuple(gathered)


def extended(block, sides, width, periodic):
    for axis, dim in sides:
        count = lax.axis_size(axis)
        forward = [(i, i + 1) for i in range(count - 1)]
        if periodic:
            forward.append((count - 1, 0))
        backward = [(target, source) for source, target in forward]
        low = lax.ppermute(
            lax.slice_in_dim(block, block.shape[dim] - width, None, axis=dim), axis, forward
        )
        high = lax.ppermute(lax.slice_in_dim(block, 0, width, axis=dim), axis, backward)
        block = jnp.concatenate([low, block, high], axis=dim)
    return block


def mode_table(azimuth):
    mode_index = jnp.arange(MODES).astype(jnp.float32)
    angles = azimuth[:, None] * mode_index[None, :]
    basis = jnp.stack([jnp.cos(angles), jnp.sin(angles)], axis=-1).reshape(
        azimuth.shape[0], 2 * MODES
    )
    slope = jnp.stack(
        [-mode_index * jnp.sin(angles), mode_index * jnp.cos(angles)], axis=-1
    ).reshape(azimuth.shape[0], 2 * MODES)
    return (basis, slope)


def radial_flux(lower_side, upper_side, sound):

    def physical(fields):
        velocity = fields[1] / fields[0]
        flux = jnp.stack(
            [fields[1], fields[1] * velocity + sound * fields[0], fields[2] * velocity]
        )
        return (flux, velocity)

    flux_lower, vel_lower = physical(lower_side)
    flux_upper, vel_upper = physical(upper_side)
    wave_speed = jnp.maximum(jnp.abs(vel_lower), jnp.abs(vel_upper)) + jnp.sqrt(sound)
    return 0.5 * (flux_lower + flux_upper) - 0.5 * wave_speed * (upper_side - lower_side)


def azimuth_flux(lower_side, upper_side, sound):

    def physical(fields):
        velocity = fields[2] / fields[0]
        flux = jnp.stack(
            [fields[2], fields[1] * velocity, fields[2] * velocity + sound * fields[0]]
        )
        return (flux, velocity)

    flux_lower, vel_lower = physical(lower_side)
    flux_upper, vel_upper = physical(upper_side)
    wave_speed = jnp.maximum(jnp.abs(vel_lower), jnp.abs(vel_upper)) + jnp.sqrt(sound)
    return 0.5 * (flux_lower + flux_upper) - 0.5 * wave_speed * (upper_side - lower_side)


def tendency(fields, radial_ext, azimuth_ext, face_radius, grav_radial, grav_azimuth, cell_step):
    inner_radius = face_radius[:-1]
    outer_radius = face_radius[1:]
    mid_radius = 0.5 * (inner_radius + outer_radius)
    cell_area = 0.5 * (outer_radius * outer_radius - inner_radius * inner_radius)
    sound_face = (aspect_sq / face_radius)[:, None]
    sound_mid = (aspect_sq / mid_radius)[:, None]
    flux_rad = radial_flux(radial_ext[:, :, :-1], radial_ext[:, :, 1:], sound_face)
    flux_azi = azimuth_flux(azimuth_ext[..., :-1], azimuth_ext[..., 1:], sound_mid)
    weighted = flux_rad * face_radius[:, None]
    divergence = (weighted[:, :, 1:] - weighted[:, :, :-1]) / cell_area[:, None]
    divergence = divergence + (flux_azi[..., 1:] - flux_azi[..., :-1]) / (
        mid_radius[:, None] * cell_step
    )
    surface_now = fields[0]
    radial_mom = fields[1]
    spin_mom = fields[2]
    centre = mid_radius[:, None]
    source_rad = (spin_mom * spin_mom / surface_now + sound_mid * surface_now) / centre
    source_rad = source_rad + surface_now * (grav_radial / cell_step - 1.0 / (centre * centre))
    source_azi = -radial_mom * spin_mom / (surface_now * centre) + surface_now * (
        grav_azimuth / cell_step
    )
    source = jnp.stack([jnp.zeros_like(surface_now), source_rad, source_azi])
    return fields + 0.1 * cell_step * (source - divergence)


def local(density, mom_r, mom_phi, potential_kernel, force_kernel):
    highest = lax.Precision.HIGHEST
    row_count = density.shape[1]
    cell_count = density.shape[2]
    mode_count = potential_kernel.shape[0]
    col_count = 2 * mode_count
    cell_step = 2.0 * math.pi / NAZ
    az_index = lax.axis_index("az")
    rad_index = lax.axis_index("rad")
    azimuth = (
        (az_index * cell_count + jnp.arange(cell_count)).astype(jnp.float32) + 0.5
    ) * cell_step
    basis, slope = mode_table(azimuth)
    surface = jnp.sum(density, axis=0)
    partial_modes = jnp.dot(surface, basis, precision=highest) / NAZ
    own_modes = sum_at_owner(partial_modes, "az", 1)
    own_pairs = own_modes.astype(jnp.bfloat16)
    portion = gathered_copies(own_pairs, "rad", 0)
    count = portion.shape[0]
    pairs = portion.reshape(count, mode_count, 2)
    pot_part = jnp.einsum(
        "krs,skc->rkc", potential_kernel, pairs, preferred_element_type=jnp.float32
    ).reshape(row_count, col_count)
    force_part = jnp.einsum(
        "krs,skc->rkc", force_kernel, pairs, preferred_element_type=jnp.float32
    ).reshape(row_count, col_count)
    basis_rows = basis.T
    slope_rows = slope.T
    portion = rows_first((pot_part, force_part), "az", (1, 1))
    potential = jnp.dot(portion[0], basis_rows, precision=highest)
    grav_radial = jnp.dot(portion[1], basis_rows, precision=highest)
    slope_sum = jnp.dot(portion[0], slope_rows, precision=highest)
    face_radius = jnp.exp(
        (rad_index * row_count + jnp.arange(row_count + 1)).astype(jnp.float32) * cell_step
    )
    mid_radius = 0.5 * (face_radius[:-1] + face_radius[1:])
    grav_azimuth = -slope_sum / mid_radius[:, None]
    fields = jnp.stack([density, mom_r, mom_phi])
    azimuth_ext = extended(fields.astype(jnp.bfloat16), (("az", 3),), 1, True).astype(fields.dtype)
    radial_halo = extended(fields.astype(jnp.bfloat16), (("rad", 2),), 1, False).astype(
        fields.dtype
    )
    inner_rim = jnp.where(rad_index == 0, fields[:, :, :1], radial_halo[:, :, :1])
    outer_rim = jnp.where(
        rad_index == lax.axis_size("rad") - 1, fields[:, :, -1:], radial_halo[:, :, -1:]
    )
    radial_ext = jnp.concatenate([inner_rim, fields, outer_rim], axis=2)
    result = tendency(
        fields, radial_ext, azimuth_ext, face_radius, grav_radial, grav_azimuth, cell_step
    )
    return (result[0], result[1], result[2], potential)


def solution(mesh):
    placed = (
        P(None, "rad", "az"),
        P(None, "rad", "az"),
        P(None, "rad", "az"),
        P("az", "rad", None),
        P("az", "rad", None),
    )
    return jax.shard_map(
        local,
        mesh=mesh,
        in_specs=placed,
        out_specs=(
            P(None, "rad", "az"),
            P(None, "rad", "az"),
            P(None, "rad", "az"),
            P("rad", "az"),
        ),
        check_vma=False,
    )
```

profile of v0, /device:TPU:32, one launch (start us, length us, event | category | flops | bytes accessed | tf_op | source)
XLA Modules:
  0.0 215.3 jit_solution(8879129993631499688)
XLA Ops:
  0.6 0.0 copy-start
  0.6 2.3 %fusion.22 = bf16[3,2,256,512]{3,2,1,0:T(8,128)(2,1)S(1)} fusion(f32[1,2,256,512]{3,2,1,0:T(8,128)} %bitcast.53, f32[1,2,256,512]{3,2,1,0:T(8,128)} %bitcast.58, f32[1,2,256,512]{3,2,1,0:T(8,128)} %bitcast.48), kind=kLoop, calls=%fused_computation.76 | loop fusion | flops 1572864 | bytes 4718592 | tf_op jit(solution)/shard_map/convert_element_type | solution.py:174
  3.0 0.0 copy-start.1
  3.0 1.1 fusion.25
  4.1 10.9 %collective-permute-start.3 = (bf16[3,2,256,1]{3,2,1,0:T(8,128)(2,1)}, bf16[3,2,256,1]{3,2,1,0:T(8,128)(2,1)}, u32[]{:S(2)}, u32[]{:S(2)}) collective-permute-start(bf16[3,2,256,1]{3,2,1,0:T(8,128)(2,1)} %get-tuple-element.34), channel_id=1, source_target_pairs={{8,0},{16,8},{24,16},{32,24},{40,32},{48,40},{56,48},{64,56},{72,6... | collective-permute-start | bytes 9224 | tf_op jit(solution)/shard_map/ppermute | solution.py:61
  15.0 0.6 fusion.24
  15.6 2.1 collective-permute-start.1
  17.7 2.3 %collective-permute-start = (bf16[3,2,1,512]{3,2,1,0:T(2,128)(2,1)}, bf16[3,2,1,512]{3,2,1,0:T(2,128)(2,1)}, u32[]{:S(2)}, u32[]{:S(2)}) collective-permute-start(bf16[3,2,1,512]{3,2,1,0:T(2,128)(2,1)} %get-tuple-element.31), channel_id=1, source_target_pairs={{0,1},{1,2},{2,3},{3,4},{4,5},{5,6},{6,7},{8,9},{9,10},{10,11},{11... | collective-permute-start | bytes 18440 | tf_op jit(solution)/shard_map/ppermute | solution.py:58
  20.0 0.5 multiply_cosine_fusion
  20.6 0.8 pad_maximum_fusion.2
  21.3 0.9 copy.10
  22.2 1.1 reshape.288
  23.4 0.9 reduce_sum.18
  24.3 1.7 convolution_multiply_fusion.1
  26.0 0.7 reshape.289
  26.7 11.8 %all-to-all-start = ((f32[32,256,4]{1,2,0:T(4,128)}), f32[32,256,4]{1,2,0:T(4,128)S(1)}, u32[]{:S(2)}, u32[]{:S(2)}) async-start(f32[32,256,4]{1,2,0:T(4,128)} %bitcast.63), calls=%async_computation | async-start | bytes 262144 | tf_op jit(solution)/shard_map/all_to_all | solution.py:19
  38.5 3.8 %pad_maximum_fusion.1 = f32[3,2,256,512]{3,2,1,0:T(8,128)} fusion(f32[1,2,256,512]{3,2,1,0:T(8,128)} %bitcast.54, f32[1,2,256,512]{3,2,1,0:T(8,128)} %bitcast.59, f32[1,2,256,512]{3,2,1,0:T(8,128)S(1)} %bitcast.49), kind=kLoop, calls=%fused_computation.19 | loop fusion | flops 1572864 | bytes 6291456 | tf_op jit(solution)/shard_map/stack | solution.py:172
  42.3 0.7 subtract_multiply_fusion
  43.0 0.5 copy-done.14
  43.5 0.6 fusion.23
  44.1 0.6 broadcast_divide_fusion
  44.7 1.9 copy.12
  46.6 1.8 reshape.292
  48.4 0.5 pad.26.clone
  49.0 2.5 %maximum_convert_fusion = f32[3,2,256,514]{3,2,1,0:T(8,128)S(1)} fusion(bf16[3,2,256,1]{3,2,1,0:T(8,128)(2,1)} %collective-permute-done.3, bf16[3,2,256,512]{3,2,1,0:T(8,128)(2,1)} %copy-done.8, bf16[3,2,256,1]{3,2,1,0:T(8,128)(2,1)} %collective-permute-done.2), kind=kLoop, calls=%fused_computation.20 | loop fusion | flops 4737024 | bytes 4737024 | tf_op jit(solution)/shard_map/convert_element_type | solution.py:173
  51.4 1.4 multiply_add_fusion
  52.9 0.0 copy-start.2
  52.9 2.5 %fusion.1 = f32[3,2,256,513]{3,2,1,0:T(8,128)} fusion(f32[3,2,256,514]{3,2,1,0:T(8,128)S(1)} %maximum_convert_fusion, f32[1,2,256,513]{3,2,1,0:T(8,128)S(1)} %get-tuple-element.11, f32[1,2,256,513]{3,2,1,0:T(8,128)S(1)} %get-tuple-element.15, f32[1,2,256,513]{3,2,1,0:T(8,128)S(1)} %get-tuple-element.16, f32[1,2,256,513]{3,2,1,0:T(8,128)S(1)} %get-tuple-element.10, ...), kind=kLoop, calls=%fused_computation.2 | loop fusion | flops 7091712 | bytes 16809984 | tf_op jit(solution)/shard_map/sub | solution.py:105
  55.4 0.6 copy-done.11
  56.0 1.0 broadcast_select_fusion
  57.0 0.0 copy-start.10
  57.1 0.8 pad_maximum_fusion
  58.0 4.3 %multiply_bitcast_fusion.1 = (f32[2,257,512]{2,1,0:T(8,128)}, f32[1,2,257,512]{3,2,1,0:T(8,128)}, f32[1,2,257,512]{3,2,1,0:T(8,128)}, f32[1,2,257,512]{3,2,1,0:T...) fusion(f32[257]{0:T(512)S(1)} %copy-done.17, ...), kind=kLoop, calls=%fused_computation.38 | loop fusion | flops 3947520 | bytes 13686792 | tf_op jit(solution)/shard_map/mul | solution.py:90
  62.3 0.6 reduce_sum.19
  62.9 1.3 broadcast_in_dim.2
  64.2 4.8 %all-to-all-start.1 = ((bf16[8,256,4]{1,2,0:T(4,128)(2,1)}), bf16[8,256,4]{1,2,0:T(4,128)(2,1)S(1)}, u32[]{:S(2)}, u32[]{:S(2)}) async-start(bf16[8,256,4]{1,2,0:T(4,128)(2,1)} %broadcast_in_dim.2), calls=%async_computation.1 | async-start | bytes 32768 | tf_op jit(solution)/shard_map/all_to_all | solution.py:31
  69.0 7.4 %fusion.5 = f32[3,2,257,512]{3,2,1,0:T(8,128)} fusion(f32[1,2,257,512]{3,2,1,0:T(8,128)} %get-tuple-element.22, f32[1,2,257,512]{3,2,1,0:T(8,128)} %get-tuple-element.19, f32[1,2,257,512]{3,2,1,0:T(8,128)} %get-tuple-element.23, f32[1,2,257,512]{3,2,1,0:T(8,128)} %get-tuple-element.20, f32[1,2,257,512]{3,2,1,0:T(8,128)} %get-tuple-element.18, ...), kind=kLoop, calls=%fused_computation.9 | loop fusion | flops 12632064 | bytes 13698052 | tf_op jit(solution)/shard_map/mul | solution.py:117
  76.5 0.6 convolution_bitcast_fusion
  77.2 2.2 %convolution_bitcast_fusion.1 = f32[256,2,2]{0,2,1:T(2,128)S(1)} fusion(bf16[2048,2,2]{0,2,1:T(2,128)(2,1)S(1)} %reshape_reshape.3, bf16[2,256,2048]{2,1,0:T(8,128)(2,1)} %param.8), kind=kOutput, calls=%fused_computation.35 | convolution fusion | flops 4194304 | bytes 2117632 | tf_op jit(solution)/shard_map/krs,skc->rkc/dot_general | solution.py:155
  79.4 122.8 %all-gather = f32[32,4,512]{2,1,0:T(4,128)} all-gather(f32[1,4,512]{2,1,0:T(4,128)S(1)} %maximum_bitcast_fusion), channel_id=1, replica_groups=mesh['az'=32,'rad'=8] {'az'}, dimensions={0}, use_global_device_ids=true | all-gather | bytes 270336 | tf_op jit(solution)/shard_map/all_gather | solution.py:43
  202.2 1.7 reshape.294
  203.9 2.5 %fusion.16 = f32[256,512]{1,0:T(8,128)} fusion(f32[512,128]{0,1:T(8,128)S(1)} %reshape.288, f32[128,512]{1,0:T(8,128)} %reshape.294), kind=kOutput, calls=%fused_computation.53 | convolution fusion | flops 201326592 | bytes 917504 | tf_op jit(solution)/shard_map/dot_general | solution.py:164
  206.4 1.5 fusion.14
  208.0 1.8 fusion.13
  209.8 0.7 add_bitcast_fusion.1
  210.6 1.3 copy-done.6
  211.8 1.7 fusion.10
  213.6 1.7 slice_bitcast_fusion
  (55 shorter events, 0.2 us)
Async XLA Ops:
  0.6 75.8 %copy-start = (bf16[2,256,2048]{2,1,0:T(8,128)(2,1)S(1)}, bf16[2,256,2048]{2,1,0:T(8,128)(2,1)}, u32[]{:S(2)}) copy-start(bf16[2,256,2048]{2,1,0:T(8,128)(2,1)} %param.9) | copy-start | bytes 6291460
  3.0 12.0 %copy-start.8 = (bf16[3,2,256,512]{3,2,1,0:T(8,128)(2,1)}, bf16[3,2,256,512]{3,2,1,0:T(8,128)(2,1)S(1)}, u32[]{:S(2)}) copy-start(bf16[3,2,256,512]{3,2,1,0:T(8,128)(2,1)S(1)} %fusion.22) | copy-start | bytes 4718596
  3.0 20.3 %copy-start.1 = (f32[2,256,512]{2,1,0:T(8,128)S(1)}, f32[2,256,512]{2,1,0:T(8,128)}, u32[]{:S(2)}) copy-start(f32[2,256,512]{2,1,0:T(8,128)} %param.5) | copy-start | bytes 3145732
  4.1 44.9 %collective-permute-start.3 = (bf16[3,2,256,1]{3,2,1,0:T(8,128)(2,1)}, bf16[3,2,256,1]{3,2,1,0:T(8,128)(2,1)}, u32[]{:S(2)}, u32[]{:S(2)}) collective-permute-start(bf16[3,2,256,1]{3,2,1,0:T(8,128)(2,1)} %get-tuple-element.34), channel_id=1, source_target_pairs={{8,0},{16,8},{24,16},{32,24},{40,32},{48,40},{56,48},{64,56},{72,6... | collective-permute-start | bytes 9224 | tf_op jit(solution)/shard_map/ppermute | solution.py:61
  15.0 33.9 %collective-permute-start.2 = (bf16[3,2,256,1]{3,2,1,0:T(8,128)(2,1)}, bf16[3,2,256,1]{3,2,1,0:T(8,128)(2,1)}, u32[]{:S(2)}, u32[]{:S(2)}) collective-permute-start(bf16[3,2,256,1]{3,2,1,0:T(8,128)(2,1)} %get-tuple-element.33), channel_id=1, source_target_pairs={{0,8},{8,16},{16,24},{24,32},{32,40},{40,48},{48,56},{56,64},{64,7... | collective-permute-start | bytes 9224 | tf_op jit(solution)/shard_map/ppermute | solution.py:58
  15.6 39.8 %collective-permute-start.1 = (bf16[3,2,1,512]{3,2,1,0:T(2,128)(2,1)}, bf16[3,2,1,512]{3,2,1,0:T(2,128)(2,1)S(1)}, u32[]{:S(2)}, u32[]{:S(2)}) collective-permute-start(bf16[3,2,1,512]{3,2,1,0:T(2,128)(2,1)} %get-tuple-element.32), channel_id=1, source_target_pairs={{1,0},{2,1},{3,2},{4,3},{5,4},{6,5},{7,6},{9,8},{10,9},{11,10},{12... | collective-permute-start | bytes 18440 | tf_op jit(solution)/shard_map/ppermute | solution.py:61
  17.7 38.3 %collective-permute-start = (bf16[3,2,1,512]{3,2,1,0:T(2,128)(2,1)}, bf16[3,2,1,512]{3,2,1,0:T(2,128)(2,1)}, u32[]{:S(2)}, u32[]{:S(2)}) collective-permute-start(bf16[3,2,1,512]{3,2,1,0:T(2,128)(2,1)} %get-tuple-element.31), channel_id=1, source_target_pairs={{0,1},{1,2},{2,3},{3,4},{4,5},{5,6},{6,7},{8,9},{9,10},{10,11},{11... | collective-permute-start | bytes 18440 | tf_op jit(solution)/shard_map/ppermute | solution.py:58
  26.7 35.6 %all-to-all-start = ((f32[32,256,4]{1,2,0:T(4,128)}), f32[32,256,4]{1,2,0:T(4,128)S(1)}, u32[]{:S(2)}, u32[]{:S(2)}) async-start(f32[32,256,4]{1,2,0:T(4,128)} %bitcast.63), calls=%async_computation | async-start | bytes 262144 | tf_op jit(solution)/shard_map/all_to_all | solution.py:19
  43.0 0.5 copy-start.14
  48.9 2.5 %copy-start.12 = (f32[256]{0:T(256)S(1)}, f32[256]{0:T(256)}, u32[]{:S(2)}) copy-start(f32[256]{0:T(256)} %get-tuple-element.7) | copy-start | bytes 3076
  48.9 2.5 %copy-start.18 = (f32[256]{0:T(256)S(1)}, f32[256]{0:T(256)}, u32[]{:S(2)}) copy-start(f32[256]{0:T(256)} %get-tuple-element.6) | copy-start | bytes 3076
  52.9 3.1 %copy-start.9 = (bf16[3,2,256,512]{3,2,1,0:T(8,128)(2,1)S(1)}, bf16[3,2,256,512]{3,2,1,0:T(8,128)(2,1)}, u32[]{:S(2)}) copy-start(bf16[3,2,256,512]{3,2,1,0:T(8,128)(2,1)} %copy-done.8) | copy-start | bytes 4718596
  52.9 4.2 %copy-start.2 = (f32[2,256,512]{2,1,0:T(8,128)S(1)}, f32[2,256,512]{2,1,0:T(8,128)}, u32[]{:S(2)}) copy-start(f32[2,256,512]{2,1,0:T(8,128)} %param.7) | copy-start | bytes 3145732
  52.9 4.2 %copy-start.4 = (f32[2,256,512]{2,1,0:T(8,128)S(1)}, f32[2,256,512]{2,1,0:T(8,128)}, u32[]{:S(2)}) copy-start(f32[2,256,512]{2,1,0:T(8,128)} %param.6) | copy-start | bytes 3145732
  55.4 0.6 copy-start.11
  57.0 0.9 copy-start.10
  57.1 0.9 copy-start.16
  57.1 0.9 copy-start.17
  64.2 12.2 %all-to-all-start.1 = ((bf16[8,256,4]{1,2,0:T(4,128)(2,1)}), bf16[8,256,4]{1,2,0:T(4,128)(2,1)S(1)}, u32[]{:S(2)}, u32[]{:S(2)}) async-start(bf16[8,256,4]{1,2,0:T(4,128)(2,1)} %broadcast_in_dim.2), calls=%async_computation.1 | async-start | bytes 32768 | tf_op jit(solution)/shard_map/all_to_all | solution.py:31
  76.4 130.0 %copy-start.21 = (f32[256]{0:T(256)S(1)}, f32[256]{0:T(256)}, u32[]{:S(2)}) copy-start(f32[256]{0:T(256)} %get-tuple-element.41) | copy-start | bytes 3076
  76.5 131.5 %copy-start.15 = (f32[256]{0:T(256)S(1)}, f32[256]{0:T(256)}, u32[]{:S(2)}) copy-start(f32[256]{0:T(256)} %copy-done.14) | copy-start | bytes 3076
  77.1 132.6 %copy-start.13 = (f32[256]{0:T(256)S(1)}, f32[256]{0:T(256)}, u32[]{:S(2)}) copy-start(f32[256]{0:T(256)} %get-tuple-element.7) | copy-start | bytes 3076
  203.9 5.9 %copy-start.3 = (f32[2,256,512]{2,1,0:T(8,128)S(1)}, f32[2,256,512]{2,1,0:T(8,128)}, u32[]{:S(2)}) copy-start(f32[2,256,512]{2,1,0:T(8,128)} %param.7) | copy-start | bytes 3145732
  203.9 5.9 %copy-start.5 = (f32[2,256,512]{2,1,0:T(8,128)S(1)}, f32[2,256,512]{2,1,0:T(8,128)}, u32[]{:S(2)}) copy-start(f32[2,256,512]{2,1,0:T(8,128)} %param.6) | copy-start | bytes 3145732
  207.9 2.6 %copy-start.7 = (f32[3,2,256,513]{3,2,1,0:T(8,128)S(1)}, f32[3,2,256,513]{3,2,1,0:T(8,128)}, u32[]{:S(2)}) copy-start(f32[3,2,256,513]{3,2,1,0:T(8,128)} %fusion.1) | copy-start | bytes 9455620
  209.8 2.0 copy-start.6
  209.8 2.0 copy-start.19
  209.8 2.0 copy-start.20
  209.8 2.0 copy-start.22
where the time goes:
time: 216 us; the launch traced here: 215 us
  blocking collectives  123 us (57%)
  other arithmetic  33.3 us (15%)
  starting transfers between devices  31.9 us (15%)
  local copies, waits for them, and re-layouts  15.9 us (7%)
  matrix products  10.4 us (5%)
    all_gather x1, blocking collectives, rows_first(): lax.all_gather(both, axis, axis=0, tiled=True)  123 us
    ppermute x2, starting transfers between devices, extended(): lax.ppermute(lax.slice_in_dim(block, 0, width, axis=dim), axis, backward)  13 us
    all_to_all x1, starting transfers between devices, sum_at_owner(): lax.all_to_all(blocks, axis, split_axis=0, concat_axis=0, tiled=True)  11.8 us
    mul x1, other arithmetic, tendency(): weighted = flux_rad * face_radius[:, None]  7.43 us
    all_to_all x1, starting transfers between devices, copy_for_each(): lax.all_to_all(jnp.broadcast_to(shard[None], (size, *shard.shape)), axis,...  4.81 us
  transfers between devices with their start and end apart: 6, of which 0 were waited for; matrix products, arithmetic and copies ran while one was open for 17% of the time, Pallas kernels for 0%

commit v1 on v0

--- a/solution.py
+++ b/solution.py
@@ -40,7 +40,13 @@
 def rows_first(arrays, axis, dims):
     turned = [jnp.moveaxis(a, dim, 0) for a, dim in zip(arrays, dims)]
     both = jnp.concatenate([t.reshape(len(t), -1) for t in turned], axis=1)
-    result, at, gathered = (lax.all_gather(both, axis, axis=0, tiled=True), 0, [])
+    result, at, gathered = (
+        jnp.concatenate(
+            lax.all_to_all(jnp.stack([both] * lax.axis_size(axis)), axis, 0, 0), axis=0
+        ),
+        0,
+        [],
+    )
     for t, dim in zip(turned, dims):
         slab = result[:, at : at + t[0].size].reshape(-1, *t.shape[1:])
         gathered.append(jnp.moveaxis(slab, 0, dim))

time: 216 us -> 121 us (0.56)
  blocking collectives: 123 us -> 0 us
  starting transfers between devices: 31.9 us -> 44.4 us
  waiting for transfers between devices: 0.02 us -> 8.46 us
  other arithmetic: 33.3 us -> 38.5 us
    all_gather x1 -> x0, blocking collectives: 123 us -> none  [rows_first(): lax.all_gather(both, axis, axis=0, tiled=True)]
    all_to_all x0 -> x1, starting transfers between devices: none -> 12.5 us  [rows_first(): lax.all_to_all(jnp.stack([both] * lax.axis_size(axis)), axis, 0, 0)]
    all_to_all x0 -> x1, waiting for transfers between devices: none -> 8.44 us  [rows_first(): lax.all_to_all(jnp.stack([both] * lax.axis_size(axis)), axis, 0, 0)]
    mul x1, other arithmetic: 4.3 us -> 7.27 us  [radial_flux(): 0.5 * wave_speed * (upper_side - lower_side)]
    concatenate x1, other arithmetic: 0.84 us -> 3.14 us  [local(): radial_ext = jnp.concatenate([inner_rim, fields, outer_rim], axis=2)]
  transfers between devices with their start and end apart: 6 -> 7, of which waited for: 0 -> 1; matrix products, arithmetic and copies ran while one was open for 17% -> 35% of each run, Pallas kernels for 0% -> 0%
where the time goes in v1:
time: 121 us; the launch traced here: 120 us
  starting transfers between devices  44.4 us (37%)
  other arithmetic  38.5 us (32%)
  local copies, waits for them, and re-layouts  17.3 us (14%)
  matrix products  10.4 us (9%)
  waiting for transfers between devices  8.46 us (7%)
    ppermute x2, starting transfers between devices, extended(): lax.ppermute(lax.slice_in_dim(block, 0, width, axis=dim), axis, backward)  13 us
    all_to_all x1, starting transfers between devices, rows_first(): lax.all_to_all(jnp.stack([both] * lax.axis_size(axis)), axis, 0, 0)  12.5 us
    all_to_all x1, starting transfers between devices, sum_at_owner(): lax.all_to_all(blocks, axis, split_axis=0, concat_axis=0, tiled=True)  11.8 us
    all_to_all x1, waiting for transfers between devices, rows_first(): lax.all_to_all(jnp.stack([both] * lax.axis_size(axis)), axis, 0, 0)  8.44 us
    mul x1, other arithmetic, tendency(): weighted = flux_rad * face_radius[:, None]  7.39 us
    mul x1, other arithmetic, radial_flux(): 0.5 * wave_speed * (upper_side - lower_side)  7.27 us
    all_to_all x1, starting transfers between devices, copy_for_each(): lax.all_to_all(jnp.broadcast_to(shard[None], (size, *shard.shape)), axis,...  4.8 us
    another operation x1, other arithmetic, local(): fields = jnp.stack([density, mom_r, mom_phi])  3.81 us
  transfers between devices with their start and end apart: 7, of which 1 were waited for; matrix products, arithmetic and copies ran while one was open for 35% of the time, Pallas kernels for 0%

profile of v1, /device:TPU:32, one launch (start us, length us, event | category | flops | bytes accessed | tf_op | source)
XLA Modules:
  0.0 120.1 jit_solution(7119657811053148488)
XLA Ops:
  0.6 0.0 copy-start
  0.6 2.3 %fusion.22 = bf16[3,2,256,512]{3,2,1,0:T(8,128)(2,1)S(1)} fusion(f32[1,2,256,512]{3,2,1,0:T(8,128)} %bitcast.51, f32[1,2,256,512]{3,2,1,0:T(8,128)} %bitcast.56, f32[1,2,256,512]{3,2,1,0:T(8,128)} %bitcast.46), kind=kLoop, calls=%fused_computation.76 | loop fusion | flops 1572864 | bytes 4718592 | tf_op jit(solution)/shard_map/convert_element_type | solution.py:180
  3.0 1.1 fusion.25
  4.1 10.9 %collective-permute-start.3 = (bf16[3,2,256,1]{3,2,1,0:T(8,128)(2,1)}, bf16[3,2,256,1]{3,2,1,0:T(8,128)(2,1)}, u32[]{:S(2)}, u32[]{:S(2)}) collective-permute-start(bf16[3,2,256,1]{3,2,1,0:T(8,128)(2,1)} %get-tuple-element.34), channel_id=1, source_target_pairs={{8,0},{16,8},{24,16},{32,24},{40,32},{48,40},{56,48},{64,56},{72,6... | collective-permute-start | bytes 9224 | tf_op jit(solution)/shard_map/ppermute | solution.py:67
  15.0 0.6 fusion.24
  15.6 2.1 %collective-permute-start.1 = (bf16[3,2,1,512]{3,2,1,0:T(2,128)(2,1)}, bf16[3,2,1,512]{3,2,1,0:T(2,128)(2,1)S(1)}, u32[]{:S(2)}, u32[]{:S(2)}) collective-permute-start(bf16[3,2,1,512]{3,2,1,0:T(2,128)(2,1)} %get-tuple-element.32), channel_id=1, source_target_pairs={{1,0},{2,1},{3,2},{4,3},{5,4},{6,5},{7,6},{9,8},{10,9},{11,10},{12... | collective-permute-start | bytes 18440 | tf_op jit(solution)/shard_map/ppermute | solution.py:67
  17.7 2.3 %collective-permute-start = (bf16[3,2,1,512]{3,2,1,0:T(2,128)(2,1)}, bf16[3,2,1,512]{3,2,1,0:T(2,128)(2,1)}, u32[]{:S(2)}, u32[]{:S(2)}) collective-permute-start(bf16[3,2,1,512]{3,2,1,0:T(2,128)(2,1)} %get-tuple-element.31), channel_id=1, source_target_pairs={{0,1},{1,2},{2,3},{3,4},{4,5},{5,6},{6,7},{8,9},{9,10},{10,11},{11... | collective-permute-start | bytes 18440 | tf_op jit(solution)/shard_map/ppermute | solution.py:64
  20.0 0.5 multiply_cosine_fusion
  20.6 0.8 pad_maximum_fusion.2
  21.3 0.9 copy.10
  22.2 1.1 reshape.293
  23.4 0.9 reduce_sum.18
  24.3 1.7 %convolution_multiply_fusion.1 = f32[256,128]{0,1:T(8,128)S(1)} fusion(f32[256,512]{1,0:T(8,128)} %reduce_sum.18, f32[512,128]{0,1:T(8,128)S(1)} %reshape.293), kind=kOutput, calls=%fused_computation.33 | convolution fusion | flops 201359360 | bytes 917504 | tf_op jit(solution)/shard_map/dot_general | solution.py:155
  26.0 0.7 reshape.294
  26.7 11.8 %all-to-all-start = ((f32[32,256,4]{1,2,0:T(4,128)}), f32[32,256,4]{1,2,0:T(4,128)S(1)}, u32[]{:S(2)}, u32[]{:S(2)}) async-start(f32[32,256,4]{1,2,0:T(4,128)} %bitcast.61), calls=%async_computation | async-start | bytes 262144 | tf_op jit(solution)/shard_map/all_to_all | solution.py:19
  38.5 3.8 %pad_maximum_fusion.1 = f32[3,2,256,512]{3,2,1,0:T(8,128)} fusion(f32[1,2,256,512]{3,2,1,0:T(8,128)} %bitcast.52, f32[1,2,256,512]{3,2,1,0:T(8,128)} %bitcast.57, f32[1,2,256,512]{3,2,1,0:T(8,128)S(1)} %bitcast.47), kind=kLoop, calls=%fused_computation.19 | loop fusion | flops 1572864 | bytes 6291456 | tf_op jit(solution)/shard_map/stack | solution.py:178
  42.3 0.7 subtract_multiply_fusion
  43.0 0.6 copy-done.15
  43.6 0.6 fusion.23
  44.2 0.6 broadcast_divide_fusion
  44.8 1.9 %copy.12 = f32[512,64,2]{0,2,1:T(2,128)} copy(f32[512,64,2]{0,1,2:T(8,128)} %get-tuple-element.46) | data formatting | bytes 524288 | tf_op jit(solution)/shard_map/stack | solution.py:78
  46.6 1.8 %reshape.298 = f32[512,128]{0,1:T(8,128)} reshape(f32[512,64,2]{0,2,1:T(2,128)} %copy.12) | data formatting | bytes 524288 | tf_op jit(solution)/shard_map/reshape | solution.py:80
  48.5 0.5 pad.26.clone
  49.0 2.5 %maximum_convert_fusion = f32[3,2,256,514]{3,2,1,0:T(8,128)S(1)} fusion(bf16[3,2,256,1]{3,2,1,0:T(8,128)(2,1)} %collective-permute-done.3, bf16[3,2,256,512]{3,2,1,0:T(8,128)(2,1)} %copy-done.8, bf16[3,2,256,1]{3,2,1,0:T(8,128)(2,1)} %collective-permute-done.2), kind=kLoop, calls=%fused_computation.20 | loop fusion | flops 4737024 | bytes 4737024 | tf_op jit(solution)/shard_map/convert_element_type | solution.py:179
  51.5 1.4 %multiply_add_fusion = (f32[1,2,256,513]{3,2,1,0:T(8,128)S(1)}, f32[1,2,256,513]{3,2,1,0:T(8,128)S(1)}, f32[2,256,513]{2,1,0:T(8,128)S(1)}, f32[1,2,256,513]{3,2...) fusion(f32[3,2,256,514]{3,2,1,0:T(8,128)S(1)} %maximum_convert_, ...), kind=kLoop, calls=%fused_computation.24 | loop fusion | flops 3939840 | bytes 13660160 | tf_op jit(solution)/shard_map/add | solution.py:104
  53.0 2.5 %fusion.1 = f32[3,2,256,513]{3,2,1,0:T(8,128)} fusion(f32[3,2,256,514]{3,2,1,0:T(8,128)S(1)} %maximum_convert_fusion, f32[1,2,256,513]{3,2,1,0:T(8,128)S(1)} %get-tuple-element.11, f32[1,2,256,513]{3,2,1,0:T(8,128)S(1)} %get-tuple-element.15, f32[1,2,256,513]{3,2,1,0:T(8,128)S(1)} %get-tuple-element.16, f32[1,2,256,513]{3,2,1,0:T(8,128)S(1)} %get-tuple-element.10, ...), kind=kLoop, calls=%fused_computation.2 | loop fusion | flops 7091712 | bytes 16809984 | tf_op jit(solution)/shard_map/sub | solution.py:111
  55.5 0.6 copy-done.12
  56.1 1.0 broadcast_select_fusion
  57.1 0.6 copy-done.10
  57.7 3.1 %pad_maximum_fusion = (f32[3,2,257,512]{3,2,1,0:T(8,128)}, f32[3,2,257,512]{3,2,1,0:T(8,128)}) fusion(f32[3,2,1,512]{3,2,1,0:T(1,128)S(1)} %get-tuple-element.8, f32[1,2,256,512]{3,2,1,0:T(8,128)S(1)} %bitcast.54, f32[1,2,256,512]{3,2,1,0:T(8,128)S(1)} %bitcast.59, f32[1,2,256,512]{3,2,1,0:T(8,128)S(1)} %bitcast.48, f32[3,2,1,512]{3,2,1,0:T(1,128)S(1)} %get-tuple-element.9), kind=kLoop, calls=%fused_computation.10 | loop fusion | flops 4737024 | bytes 9486336 | tf_op jit(solution)/shard_map/concatenate | solution.py:187
  60.9 0.6 reduce_sum.19
  61.5 1.3 %broadcast_in_dim.2 = bf16[8,256,4]{1,2,0:T(4,128)(2,1)} broadcast(bf16[256,4]{0,1:T(4,128)(2,1)} %reduce_sum.19), dimensions={1,2} | broadcast | bytes 18432 | tf_op jit(solution)/shard_map/broadcast_in_dim | solution.py:32
  62.8 4.8 %all-to-all-start.1 = ((bf16[8,256,4]{1,2,0:T(4,128)(2,1)}), bf16[8,256,4]{1,2,0:T(4,128)(2,1)S(1)}, u32[]{:S(2)}, u32[]{:S(2)}) async-start(bf16[8,256,4]{1,2,0:T(4,128)(2,1)} %broadcast_in_dim.2), calls=%async_computation.1 | async-start | bytes 32768 | tf_op jit(solution)/shard_map/all_to_all | solution.py:31
  67.6 7.3 %multiply_bitcast_fusion.1 = (f32[2,257,512]{2,1,0:T(8,128)}, f32[1,2,257,512]{3,2,1,0:T(8,128)}, f32[1,2,257,512]{3,2,1,0:T(8,128)}, f32[1,2,257,512]{3,2,1,0:T...) fusion(f32[257]{0:T(512)} %get-tuple-element.44, ...), kind=kLoop, calls=%fused_computation.38 | loop fusion | flops 3947520 | bytes 13686792 | tf_op jit(solution)/shard_map/mul | solution.py:96
  74.9 0.6 convolution_bitcast_fusion
  75.6 2.2 %convolution_bitcast_fusion.1 = f32[256,2,2]{0,2,1:T(2,128)S(1)} fusion(bf16[2048,2,2]{0,2,1:T(2,128)(2,1)S(1)} %reshape_reshape.3, bf16[2,256,2048]{2,1,0:T(8,128)(2,1)} %param.8), kind=kOutput, calls=%fused_computation.35 | convolution fusion | flops 4194304 | bytes 2117632 | tf_op jit(solution)/shard_map/krs,skc->rkc/dot_general | solution.py:161
  77.8 0.7 stack.33
  78.6 12.5 %all-to-all-start.2 = ((f32[32,4,512]{2,1,0:T(4,128)}), f32[32,4,512]{2,1,0:T(4,128)}, u32[]{:S(2)}, u32[]{:S(2)}) async-start(f32[32,4,512]{2,1,0:T(4,128)} %stack.33), calls=%async_computation.2 | async-start | bytes 524288 | tf_op jit(solution)/shard_map/all_to_all | solution.py:45
  91.2 7.4 %fusion.5 = f32[3,2,257,512]{3,2,1,0:T(8,128)} fusion(f32[1,2,257,512]{3,2,1,0:T(8,128)} %get-tuple-element.22, f32[1,2,257,512]{3,2,1,0:T(8,128)} %get-tuple-element.19, f32[1,2,257,512]{3,2,1,0:T(8,128)} %get-tuple-element.23, f32[1,2,257,512]{3,2,1,0:T(8,128)} %get-tuple-element.20, f32[1,2,257,512]{3,2,1,0:T(8,128)} %get-tuple-element.18, ...), kind=kLoop, calls=%fused_computation.9 | loop fusion | flops 12632064 | bytes 13698052 | tf_op jit(solution)/shard_map/mul | solution.py:123
  98.6 8.4 %all-to-all-done.2 = f32[32,4,512]{2,1,0:T(4,128)} async-done(((f32[32,4,512]{2,1,0:T(4,128)}), f32[32,4,512]{2,1,0:T(4,128)}, u32[]{:S(2)}, u32[]{:S(2)}) %all-to-all-start.2) | async-done | bytes 262176 | tf_op jit(solution)/shard_map/all_to_all | solution.py:45
  107.0 1.7 %reshape.297 = f32[128,512]{1,0:T(8,128)} reshape(f32[32,4,512]{2,1,0:T(4,128)} %all-to-all-done.2) | data formatting | bytes 524288 | tf_op jit(solution)/shard_map/reshape | solution.py:44
  108.8 2.5 %fusion.16 = f32[256,512]{1,0:T(8,128)} fusion(f32[512,128]{0,1:T(8,128)S(1)} %reshape.293, f32[128,512]{1,0:T(8,128)} %reshape.297), kind=kOutput, calls=%fused_computation.53 | convolution fusion | flops 201326592 | bytes 917504 | tf_op jit(solution)/shard_map/dot_general | solution.py:170
  111.2 1.5 %fusion.14 = f32[256,512]{1,0:T(8,128)S(1)} fusion(f32[512,128]{0,1:T(8,128)S(1)} %reshape.293, f32[256]{0:T(256)S(1)} %copy-done.20, f32[128,512]{1,0:T(8,128)} %reshape.297), kind=kOutput, calls=%fused_computation.30 | convolution fusion | flops 201588736 | bytes 918528 | tf_op jit(solution)/shard_map/dot_general | solution.py:171
  112.8 1.8 %fusion.13 = f32[256,512]{1,0:T(8,128)S(1)} fusion(f32[512,128]{0,1:T(8,128)} %reshape.298, f32[256]{0:T(256)S(1)} %copy-done.16, f32[128,512]{1,0:T(8,128)} %reshape.297), kind=kOutput, calls=%fused_computation.28 | convolution fusion | flops 201719808 | bytes 918528 | tf_op jit(solution)/shard_map/dot_general | solution.py:172
  114.7 0.7 add_bitcast_fusion.1
  115.4 1.3 %copy-done.6 = f32[3,2,257,512]{3,2,1,0:T(8,128)S(1)} copy-done((f32[3,2,257,512]{3,2,1,0:T(8,128)S(1)}, f32[3,2,257,512]{3,2,1,0:T(8,128)}, u32[]{:S(2)}) %copy-start.6) | copy-done | bytes 3158040
  116.7 1.7 %fusion.10 = f32[3,2,256,512]{3,2,1,0:T(8,128)S(1)} fusion(f32[3,2,256,513]{3,2,1,0:T(8,128)S(1)} %copy-done.7, f32[3,2,257,512]{3,2,1,0:T(8,128)S(1)} %copy-done.6, f32[1,2,256,512]{3,2,1,0:T(8,128)S(1)} %get-tuple-element.30, f32[1,2,256,512]{3,2,1,0:T(8,128)S(1)} %get-tuple-element.29, f32[3]{0:T(128)S(1)} %copy-done.21, f32[256]{0:T(256)S(1)} %copy-done.19, ...), kind=kLoop, calls=%fused_computation.16 | loop fusion | flops 9437184 | bytes 20973580 | tf_op jit(solution)/shard_map/add | solution.py:138
  118.4 1.7 %slice_bitcast_fusion = (f32[2,256,512]{2,1,0:T(8,128)}, f32[2,256,512]{2,1,0:T(8,128)}, f32[2,256,512]{2,1,0:T(8,128)}) fusion(f32[3,2,256,512]{3,2,1,0:T(8,128)S(1)} %fusion.10), kind=kLoop, calls=%fused_computation.41 | loop fusion | bytes 6291456 | tf_op jit(solution)/shard_map/squeeze | solution.py:191
  (55 shorter events, 0.2 us)
Async XLA Ops:
  0.6 74.3 %copy-start = (bf16[2,256,2048]{2,1,0:T(8,128)(2,1)S(1)}, bf16[2,256,2048]{2,1,0:T(8,128)(2,1)}, u32[]{:S(2)}) copy-start(bf16[2,256,2048]{2,1,0:T(8,128)(2,1)} %param.9) | copy-start | bytes 6291460
  3.0 12.0 %copy-start.8 = (bf16[3,2,256,512]{3,2,1,0:T(8,128)(2,1)}, bf16[3,2,256,512]{3,2,1,0:T(8,128)(2,1)S(1)}, u32[]{:S(2)}) copy-start(bf16[3,2,256,512]{3,2,1,0:T(8,128)(2,1)S(1)} %fusion.22) | copy-start | bytes 4718596
  3.0 20.3 %copy-start.1 = (f32[2,256,512]{2,1,0:T(8,128)S(1)}, f32[2,256,512]{2,1,0:T(8,128)}, u32[]{:S(2)}) copy-start(f32[2,256,512]{2,1,0:T(8,128)} %param.5) | copy-start | bytes 3145732
  4.1 44.9 %collective-permute-start.3 = (bf16[3,2,256,1]{3,2,1,0:T(8,128)(2,1)}, bf16[3,2,256,1]{3,2,1,0:T(8,128)(2,1)}, u32[]{:S(2)}, u32[]{:S(2)}) collective-permute-start(bf16[3,2,256,1]{3,2,1,0:T(8,128)(2,1)} %get-tuple-element.34), channel_id=1, source_target_pairs={{8,0},{16,8},{24,16},{32,24},{40,32},{48,40},{56,48},{64,56},{72,6... | collective-permute-start | bytes 9224 | tf_op jit(solution)/shard_map/ppermute | solution.py:67
  15.0 34.0 %collective-permute-start.2 = (bf16[3,2,256,1]{3,2,1,0:T(8,128)(2,1)}, bf16[3,2,256,1]{3,2,1,0:T(8,128)(2,1)}, u32[]{:S(2)}, u32[]{:S(2)}) collective-permute-start(bf16[3,2,256,1]{3,2,1,0:T(8,128)(2,1)} %get-tuple-element.33), channel_id=1, source_target_pairs={{0,8},{8,16},{16,24},{24,32},{32,40},{40,48},{48,56},{56,64},{64,7... | collective-permute-start | bytes 9224 | tf_op jit(solution)/shard_map/ppermute | solution.py:64
  15.6 39.8 %collective-permute-start.1 = (bf16[3,2,1,512]{3,2,1,0:T(2,128)(2,1)}, bf16[3,2,1,512]{3,2,1,0:T(2,128)(2,1)S(1)}, u32[]{:S(2)}, u32[]{:S(2)}) collective-permute-start(bf16[3,2,1,512]{3,2,1,0:T(2,128)(2,1)} %get-tuple-element.32), channel_id=1, source_target_pairs={{1,0},{2,1},{3,2},{4,3},{5,4},{6,5},{7,6},{9,8},{10,9},{11,10},{12... | collective-permute-start | bytes 18440 | tf_op jit(solution)/shard_map/ppermute | solution.py:67
  17.7 38.4 %collective-permute-start = (bf16[3,2,1,512]{3,2,1,0:T(2,128)(2,1)}, bf16[3,2,1,512]{3,2,1,0:T(2,128)(2,1)}, u32[]{:S(2)}, u32[]{:S(2)}) collective-permute-start(bf16[3,2,1,512]{3,2,1,0:T(2,128)(2,1)} %get-tuple-element.31), channel_id=1, source_target_pairs={{0,1},{1,2},{2,3},{3,4},{4,5},{5,6},{6,7},{8,9},{9,10},{10,11},{11... | collective-permute-start | bytes 18440 | tf_op jit(solution)/shard_map/ppermute | solution.py:64
  26.7 34.2 %all-to-all-start = ((f32[32,256,4]{1,2,0:T(4,128)}), f32[32,256,4]{1,2,0:T(4,128)S(1)}, u32[]{:S(2)}, u32[]{:S(2)}) async-start(f32[32,256,4]{1,2,0:T(4,128)} %bitcast.61), calls=%async_computation | async-start | bytes 262144 | tf_op jit(solution)/shard_map/all_to_all | solution.py:19
  43.0 0.6 copy-start.15
  49.0 2.5 %copy-start.13 = (f32[256]{0:T(256)S(1)}, f32[256]{0:T(256)}, u32[]{:S(2)}) copy-start(f32[256]{0:T(256)} %get-tuple-element.7) | copy-start | bytes 3076
  49.0 2.5 %copy-start.17 = (f32[256]{0:T(256)S(1)}, f32[256]{0:T(256)}, u32[]{:S(2)}) copy-start(f32[256]{0:T(256)} %get-tuple-element.6) | copy-start | bytes 3076
  52.9 3.1 %copy-start.9 = (bf16[3,2,256,512]{3,2,1,0:T(8,128)(2,1)S(1)}, bf16[3,2,256,512]{3,2,1,0:T(8,128)(2,1)}, u32[]{:S(2)}) copy-start(bf16[3,2,256,512]{3,2,1,0:T(8,128)(2,1)} %copy-done.8) | copy-start | bytes 4718596
  52.9 4.8 %copy-start.2 = (f32[2,256,512]{2,1,0:T(8,128)S(1)}, f32[2,256,512]{2,1,0:T(8,128)}, u32[]{:S(2)}) copy-start(f32[2,256,512]{2,1,0:T(8,128)} %param.7) | copy-start | bytes 3145732
  53.0 4.8 %copy-start.4 = (f32[2,256,512]{2,1,0:T(8,128)S(1)}, f32[2,256,512]{2,1,0:T(8,128)}, u32[]{:S(2)}) copy-start(f32[2,256,512]{2,1,0:T(8,128)} %param.6) | copy-start | bytes 3145732
  55.5 0.6 copy-start.12
  57.1 0.6 copy-start.10
  62.8 12.1 %all-to-all-start.1 = ((bf16[8,256,4]{1,2,0:T(4,128)(2,1)}), bf16[8,256,4]{1,2,0:T(4,128)(2,1)S(1)}, u32[]{:S(2)}, u32[]{:S(2)}) async-start(bf16[8,256,4]{1,2,0:T(4,128)(2,1)} %broadcast_in_dim.2), calls=%async_computation.1 | async-start | bytes 32768 | tf_op jit(solution)/shard_map/all_to_all | solution.py:31
  74.8 16.3 %copy-start.11 = (f32[3,2,1,512]{3,2,1,0:T(1,128)S(1)}, f32[3,2,1,512]{3,2,1,0:T(1,128)}, u32[]{:S(2)}) copy-start(f32[3,2,1,512]{3,2,1,0:T(1,128)} %copy-done.10) | copy-start | bytes 36868
  78.6 28.4 %all-to-all-start.2 = ((f32[32,4,512]{2,1,0:T(4,128)}), f32[32,4,512]{2,1,0:T(4,128)}, u32[]{:S(2)}, u32[]{:S(2)}) async-start(f32[32,4,512]{2,1,0:T(4,128)} %stack.33), calls=%async_computation.2 | async-start | bytes 524288 | tf_op jit(solution)/shard_map/all_to_all | solution.py:45
  91.1 20.1 %copy-start.20 = (f32[256]{0:T(256)S(1)}, f32[256]{0:T(256)}, u32[]{:S(2)}) copy-start(f32[256]{0:T(256)} %get-tuple-element.41) | copy-start | bytes 3076
  91.2 21.6 %copy-start.16 = (f32[256]{0:T(256)S(1)}, f32[256]{0:T(256)}, u32[]{:S(2)}) copy-start(f32[256]{0:T(256)} %copy-done.15) | copy-start | bytes 3076
  98.6 16.0 %copy-start.14 = (f32[256]{0:T(256)S(1)}, f32[256]{0:T(256)}, u32[]{:S(2)}) copy-start(f32[256]{0:T(256)} %get-tuple-element.7) | copy-start | bytes 3076
  108.7 5.9 %copy-start.3 = (f32[2,256,512]{2,1,0:T(8,128)S(1)}, f32[2,256,512]{2,1,0:T(8,128)}, u32[]{:S(2)}) copy-start(f32[2,256,512]{2,1,0:T(8,128)} %param.7) | copy-start | bytes 3145732
  108.8 5.9 %copy-start.5 = (f32[2,256,512]{2,1,0:T(8,128)S(1)}, f32[2,256,512]{2,1,0:T(8,128)}, u32[]{:S(2)}) copy-start(f32[2,256,512]{2,1,0:T(8,128)} %param.6) | copy-start | bytes 3145732
  112.8 2.6 %copy-start.7 = (f32[3,2,256,513]{3,2,1,0:T(8,128)S(1)}, f32[3,2,256,513]{3,2,1,0:T(8,128)}, u32[]{:S(2)}) copy-start(f32[3,2,256,513]{3,2,1,0:T(8,128)} %fusion.1) | copy-start | bytes 9455620
  114.6 2.0 %copy-start.6 = (f32[3,2,257,512]{3,2,1,0:T(8,128)S(1)}, f32[3,2,257,512]{3,2,1,0:T(8,128)}, u32[]{:S(2)}) copy-start(f32[3,2,257,512]{3,2,1,0:T(8,128)} %fusion.5) | copy-start | bytes 9474052
  114.6 2.0 %copy-start.18 = (f32[256]{0:T(256)S(1)}, f32[256]{0:T(256)}, u32[]{:S(2)}) copy-start(f32[256]{0:T(256)} %get-tuple-element.39) | copy-start | bytes 3076
  114.6 2.0 %copy-start.19 = (f32[256]{0:T(256)S(1)}, f32[256]{0:T(256)}, u32[]{:S(2)}) copy-start(f32[256]{0:T(256)} %get-tuple-element.40) | copy-start | bytes 3076
  114.7 2.0 %copy-start.21 = (f32[3]{0:T(128)S(1)}, f32[3]{0:T(128)}, u32[]{:S(2)}) copy-start(f32[3]{0:T(128)} %pad.26.clone) | copy-start | bytes 40
